TPU v7x, 128 devices: a whole 4x4x4 slice. The times are simulated.
128 devices in a mesh: gx: 4 (over z), gy: 4 (over y_hi, core), gz: 8 (over y_lo, x).
Axes of the slice: x: 4, y: 4 (y_hi: 2, y_lo: 2; y = y_hi * 2 + y_lo), z: 4, core: 2. Of those that a mesh axis runs over, the one named last changes fastest.
Arguments:
- wavefunctions: float32 [28, 28, 112, 128], P('gx', 'gy', 'gz'), may hold values from -6 to 6
- hamiltonians: float32 [4, 4, 16, 512, 512], P('gx', 'gy', 'gz'), as said below
- cell_order: int32 [4, 4, 16, 512], P('gx', 'gy', 'gz'), may hold values from 0 to 511, each once within a row
Outputs:
- rotated: float32 [28, 28, 112, 128], P('gx', 'gy', 'gz')
Inputs may be any that keep to these rules, and one draw needn't show every extreme that they name: `cell_order`: each cell's row holds every lattice position of the cell once. `hamiltonians`: each cell's matrix is symmetric.
All inputs are finite; a program needn't handle non-finite values.
Results may differ from a plain program's by a relative error of at most 0.00014.
Values sent between devices are 32-bit elements; how exact they have to be, the bound alone decides.
A program may use at most 64 MiB of HBM per device.

v0:
```python
import functools
import itertools

import jax
import jax.numpy as jnp
from jax import lax
from jax.experimental import pallas as pl
from jax.experimental.pallas import tpu as pltpu
from jax.sharding import PartitionSpec as P

NPE = 8
CDOF = 512
STATES = 128
DEGREE = 6
NS_STEPS = 12
CENTER = 0.4
HALF_WIDTH = 0.7
AXES = ("gx", "gy", "gz")
MESH = pl.DeviceIdType.MESH
F32 = jnp.float32
BF16 = jnp.bfloat16

ALL = sorted(
    (d for d in itertools.product((-1, 0, 1), repeat=3) if any(d)),
    key=lambda d: -sum(map(abs, d)),
)
DOWN = [d for d in itertools.product((-1, 0), repeat=3) if any(d)]
UP = [d for d in itertools.product((1, 0), repeat=3) if any(d)]

KINDS = ("x", "z", "xz", "y", "xy", "yz", "xyz")
Y_ROWS, X_ROWS = 0, 128
INNER = 36 * 8
SENT = 64 + 128 + 96
ROWS = SENT + INNER
EARLY, LATE = 384, 256


def split(value):
    high = value.astype(BF16)
    low = (value - high.astype(F32)).astype(BF16)
    return high, low


def product(left, right):
    columns = right.shape[1]
    high, low = split(right)
    upper = jnp.concatenate([high, low], axis=1)
    lower = jnp.concatenate([high, jnp.zeros_like(low)], axis=1)
    sums = jnp.dot(
        jnp.concatenate(split(left), axis=1),
        jnp.concatenate([upper, lower], axis=0),
        preferred_element_type=F32,
    )
    return sums[:, :columns] + sums[:, columns:]


def side(step):
    return (step + 1) // 2


def kind_of(d):
    return "".join(name for name, step in zip("xyz", d) if step)


def kernel(
    sizes,
    wave_hbm,
    ham_hbm,
    order_hbm,
    out_ref,
    wave_ref,
    ham_raw,
    pick,
    early_columns,
    late_columns,
    order_ref,
    ham_early,
    ham_sent,
    ham_inner,
    early,
    field,
    rims,
    faces,
    inner,
    yz_pack,
    r_x,
    r_y,
    r_z,
    r_xy,
    r_xz,
    r_yz,
    r_xyz,
    gram,
    r_scatter,
    r_reduce,
    r_gather,
    load_sem,
    send_sem,
    recv_sem,
    sum_send,
    sum_recv,
):
    me = tuple(lax.axis_index(a) for a in AXES)
    nx, ny, nz = sizes
    received = dict(x=r_x, y=r_y, z=r_z, xy=r_xy, xz=r_xz, yz=r_yz, xyz=r_xyz)

    shifted = [
        {s: lax.rem(m + (s + n), n) for s in (-1, 0, 1)} for m, n in zip(me, sizes)
    ]
    neighbours = {
        d: tuple(table[s] for table, s in zip(shifted, d)) for d in ALL
    }

    def neighbour(d):
        return neighbours[d]

    ring_place = me[0] * 2 + lax.rem(me[1], 2)
    other_place = (me[1] // 2) * nz + me[2]
    ring, others = nx * 2, (ny // 2) * nz

    def in_ring(j):
        place = lax.rem(ring_place + j, ring)
        return (place // 2, (me[1] // 2) * 2 + lax.rem(place, 2), me[2])

    def across(j):
        place = lax.rem(other_place + j, others)
        return (me[0], (place // nz) * 2 + lax.rem(me[1], 2), lax.rem(place, nz))

    barrier = pltpu.get_barrier_semaphore()
    for d in UP + DOWN:
        pl.semaphore_signal(barrier, inc=1, device_id=neighbour(d), device_id_type=MESH)

    loads = [
        pltpu.make_async_copy(wave_hbm, wave_ref, load_sem.at[0]),
        pltpu.make_async_copy(order_hbm, order_ref, load_sem.at[1]),
        pltpu.make_async_copy(ham_hbm.at[0], ham_raw.at[0], load_sem.at[2]),
        pltpu.make_async_copy(ham_hbm.at[1], ham_raw.at[1], load_sem.at[3]),
    ]
    for load in loads:
        load.start()

    def message(d, slot):
        dx, dy, dz = d
        kind = kind_of(d)
        sx, sy, sz = side(dx), side(dy), side(dz)
        if kind == "x":
            source, place = faces.at[:, pl.ds(X_ROWS + sx * 64, 64)], sx
        elif kind == "y":
            source, place = faces.at[:, pl.ds(Y_ROWS + sy * 64, 64)], sy
        elif kind == "z":
            source, place = rims.at[sz, pl.ds(0, 64)], sz
        elif kind == "xy":
            source = faces.at[:, pl.ds(X_ROWS + sx * 64 + sy * 56, 8)]
            place = sx * 2 + sy
        elif kind == "xz":
            source = rims.at[sz, pl.ds(sx * 56, 8)]
            place = sx * 2 + sz
        elif kind == "yz":
            source, place = yz_pack.at[sy, sz], sy * 2 + sz
        else:
            source = rims.at[sz, pl.ds(sx * 56 + sy * 7, 1)]
            place = sx * 4 + sy * 2 + sz
        if kind == "xyz":
            target = r_xyz.at[slot, pl.ds(place, 1)]
        else:
            target = received[kind].at[slot, place]
        k = KINDS.index(kind)
        return pltpu.make_async_remote_copy(
            src_ref=source,
            dst_ref=target,
            send_sem=send_sem.at[k],
            recv_sem=recv_sem.at[slot, place if kind == "y" else 2 + k],
            device_id=neighbour(d),
            device_id_type=MESH,
        )

    def send(directions, slot):
        for d in directions:
            message(d, slot).start()

    def every(kind, directions, slot):
        count = sum(kind_of(d) == kind for d in directions)
        whole = received[kind].at[slot, pl.ds(0, count)]
        k = KINDS.index(kind)
        return pltpu.make_async_remote_copy(
            src_ref=whole,
            dst_ref=whole,
            send_sem=send_sem.at[k],
            recv_sem=recv_sem.at[slot, 2 + k],
            device_id=neighbour((1, 0, 0)),
            device_id_type=MESH,
        )

    def wait_sent(directions, slot):
        for kind in KINDS:
            every(kind, directions, slot).wait_send()

    def collect_y(total, slot, place, scale):
        pltpu.make_async_remote_copy(
            src_ref=r_y.at[slot, place],
            dst_ref=r_y.at[slot, place],
            send_sem=send_sem.at[KINDS.index("y")],
            recv_sem=recv_sem.at[slot, place],
            device_id=neighbour((1, 0, 0)),
            device_id_type=MESH,
        ).wait_recv()
        for x in range(NPE):
            rows = pl.ds(pl.multiple_of(x * 64 + 56 * (1 - place), 8), 8)
            total[:, rows, :] += scale * r_y[slot, place, :, x * 8 : x * 8 + 8, :]

    def collect(total, directions, slot, scale):
        for kind in KINDS:
            if kind == "y":
                for d in directions:
                    if kind_of(d) == "y":
                        collect_y(total, slot, side(d[1]), scale)
                continue
            every(kind, directions, slot).wait_recv()
            for dx, dy, dz in directions:
                if kind_of((dx, dy, dz)) != kind:
                    continue
                sx, sy, sz = side(dx), side(dy), side(dz)
                ix, iy = 7 * (1 - sx), 7 * (1 - sy)
                c, iz = (0, 0) if dz > 0 else (1, 7)
                if kind == "x":
                    total[:, ix * 64 : ix * 64 + 64, :] += scale * r_x[slot, sx]
                elif kind == "xy":
                    row = (ix * NPE + iy) * NPE
                    total[:, row : row + 8, :] += scale * r_xy[slot, sx * 2 + sy]
                elif kind == "z":
                    total[c, pl.ds(iz, 64, stride=8), :] += scale * r_z[slot, sz]
                elif kind == "xz":
                    rows = pl.ds(ix * 64 + iz, 8, stride=8)
                    total[c, rows, :] += scale * r_xz[slot, sx * 2 + sz]
                elif kind == "yz":
                    rows = pl.ds(iy * 8 + iz, 8, stride=64)
                    total[c, rows, :] += scale * r_yz[slot, sy * 2 + sz]
                else:
                    row = (ix * NPE + iy) * NPE + iz
                    place = sx * 4 + sy * 2 + sz
                    total[c, row : row + 1, :] += scale * r_xyz[slot, place : place + 1, :]

    def pack_yz():
        for s in range(2):
            for t in range(2):
                yz_pack[t, s] = rims[s, pl.ds(7 * t, 8, stride=8), :]

    loads[0].wait()
    field[0] = jnp.zeros((2, CDOF, STATES), F32)
    for x in range(NPE - 1):
        for y in range(NPE - 1):
            row = (x * NPE + y) * NPE
            field[0, 0, row : row + 8, :] = wave_ref[x, y, 0:8, :]
            field[0, 1, row : row + 7, :] = wave_ref[x, y, 7:14, :]
    rims[0] = field[0, 0, pl.ds(0, 64, stride=8), :]
    for c in range(2):
        faces[c, X_ROWS : X_ROWS + 64, :] = field[0, c, 0:64, :]
        for x in range(NPE):
            faces[c, Y_ROWS + x * 8 : Y_ROWS + x * 8 + 8, :] = field[0, c, x * 64 : x * 64 + 8, :]
    yz_pack[0, 0] = rims[0, pl.ds(0, 8, stride=8), :]
    loads[1].wait()
    near_place = lax.rem(me[1], 2)
    near_y = 7 * (1 - near_place)
    row_of = lax.broadcasted_iota(jnp.int32, (CDOF, CDOF), 0)
    n = lax.broadcasted_iota(jnp.int32, (64, CDOF), 0)
    for c in range(2):
        order = order_ref[c : c + 1, :]

        def chosen(rows):
            return (rows == order).astype(F32).astype(BF16)

        block = (n // 8) * 64 + lax.rem(n, 8)
        rows = [n * 8 + 7 * c, block, block + 56, n[8:56], n[8:56] + 448]
        rows += [row_of[x * 64 + 8 : x * 64 + 56] for x in range(1, NPE - 1)]
        pick[c] = chosen(jnp.concatenate(rows, axis=0))
        k = lax.broadcasted_iota(jnp.int32, (48, CDOF), 0)
        none = jnp.full((48, CDOF), -1, jnp.int32)
        near_rows = (k // 8 + 1) * 64 + near_y * 8 + lax.rem(k, 8)
        early_rows = [row_of[x * 64 + 8 : x * 64 + 56] for x in range(1, NPE - 1)]
        early_rows = [
            jnp.where(lax.rem(k, 8) == 7 * c, -1, rows) for rows in early_rows + [near_rows]
        ] + [none]
        rim_rows = (k // 8 + 1) * 64 + lax.rem(k, 8) * 8 + 7 * c
        late_rows = [
            n,
            n + 448,
            (k // 8 + 1) * 64 + (7 - near_y) * 8 + lax.rem(k, 8),
            jnp.where(lax.rem(k, 8) == 7 - near_y, -1, rim_rows),
            none[:32],
        ]
        early_columns[c] = chosen(jnp.concatenate(early_rows, axis=0))
        late_columns[c] = chosen(jnp.concatenate(late_rows, axis=0))

    pl.semaphore_wait(barrier, len(UP + DOWN))
    send(DOWN, 0)

    for c in range(2):
        loads[2 + c].wait()
        for part, value in enumerate(split(ham_raw[c])):
            half = jnp.dot(pick[c], value, preferred_element_type=F32).astype(BF16)
            whole = lax.dot_general(
                half, early_columns[c], (((1,), (1,)), ((), ())), preferred_element_type=F32
            ).astype(BF16)
            ham_early[c, part * ROWS : (part + 1) * ROWS, :] = whole
            whole = lax.dot_general(
                half, late_columns[c], (((1,), (1,)), ((), ())), preferred_element_type=F32
            ).astype(BF16)
            ham_sent[c, part * SENT : (part + 1) * SENT, :] = whole[:SENT]
            ham_inner[c, part * INNER : (part + 1) * INNER, :] = whole[SENT:]


    def four(matrix, value):
        rows = matrix.shape[0] // 2
        all_four = jnp.dot(matrix, value, preferred_element_type=F32)
        return (
            all_four[:rows, :STATES]
            + (all_four[:rows, STATES:] + all_four[rows:, :STATES])
            + all_four[rows:, STATES:]
        )

    def join(ref, first, count):
        upper, lower = pl.ds(first + 7, count, stride=8), pl.ds(first, count, stride=8)
        middle = ref[0, upper, :] + ref[1, lower, :]
        ref[0, upper, :] = middle
        ref[1, lower, :] = middle

    def pair(parts):
        return jnp.concatenate(split(jnp.concatenate(parts, axis=0)), axis=1)

    def y_rows(now, c, y):
        return [
            field[now, c, pl.ds(pl.multiple_of(x * 64 + y * 8, 8), 8), :]
            for x in range(1, NPE - 1)
        ]

    def multiply_early(now):
        for c in range(2):
            parts = [field[now, c, x * 64 + 8 : x * 64 + 56, :] for x in range(1, NPE - 1)]
            parts += y_rows(now, c, near_y) + [jnp.zeros((48, STATES), F32)]
            early[c] = four(ham_early[c], pair(parts))

    def late_values(now, c):
        parts = [field[now, c, 0:64, :], field[now, c, 448:512, :]]
        parts += y_rows(now, c, 7 - near_y)
        parts += [field[now, c, pl.ds(64 + 7 * c, 48, stride=8), :]]
        return pair(parts + [jnp.zeros((32, STATES), F32)])

    def apply(now, directions, factor, keep):
        later = slot = 1 - now
        gain, shift = factor / HALF_WIDTH, -factor * CENTER / HALF_WIDTH
        values = [late_values(now, c) for c in range(2)]
        for c in range(2):
            products = early[c, :SENT, :] + four(ham_sent[c], values[c])
            rims[c] = products[:64]
            faces[c, Y_ROWS : Y_ROWS + 128, :] = products[64:192]
            for t in range(2):
                row = X_ROWS + t * 64
                faces[c, row + 8 : row + 56, :] = products[192 + t * 48 : 240 + t * 48]
                for u in range(2):
                    edge = products[64 + u * 64 + t * 56 : 72 + u * 64 + t * 56]
                    faces[c, row + u * 56 : row + u * 56 + 8, :] = edge
        pack_yz()
        join(faces, 0, 32)
        send(directions, slot)
        for c in range(2):
            inner[c, :INNER, :] = early[c, SENT:, :] + four(ham_inner[c], values[c])
        join(inner, 0, 36)

        def advance(c, row, count, products):
            rows = slice(row, row + count)
            fresh = gain * products + shift * field[now, c, rows, :]
            if keep:
                fresh = fresh - field[later, c, rows, :]
            field[later, c, rows, :] = fresh

        for c in range(2):
            for x in range(NPE):
                if x in (0, NPE - 1):
                    first = X_ROWS + 64 * (x // 7)
                    advance(c, x * 64, 64, faces[c, first : first + 64, :])
                    continue
                for t in range(2):
                    first = Y_ROWS + 64 * t + x * 8
                    advance(c, x * 64 + 56 * t, 8, faces[c, first : first + 8, :])
                first = (x - 1) * 48
                advance(c, x * 64 + 8, 48, inner[c, first : first + 48, :])
        total = field.at[later]
        if directions is ALL:
            collect_y(total, slot, near_place, gain)
            multiply_early(later)
            collect(total, [d for d in ALL if kind_of(d) != "y"], slot, gain)
            collect_y(total, slot, 1 - near_place, gain)
        else:
            collect(total, directions, slot, gain)
        wait_sent(directions, slot)

    @pl.when(near_place == 0)
    def _():
        collect_y(field.at[0], 0, 0, 1.0)

    multiply_early(0)
    collect(field.at[0], [d for d in DOWN if kind_of(d) != "y"], 0, 1.0)

    @pl.when(near_place == 1)
    def _():
        collect_y(field.at[0], 0, 0, 1.0)

    wait_sent(DOWN, 0)
    apply(0, ALL, 1.0, False)

    def two_steps(k, carry):
        apply(1, ALL, 2.0, True)
        apply(0, ALL, 2.0, True)
        return carry

    lax.fori_loop(0, (DEGREE - 2) // 2, two_steps, 0)
    apply(1, UP, 2.0, True)
    last = 0

    owned_z = lax.broadcasted_iota(jnp.int32, (7 * 8, STATES), 0) % 8 < 7
    blocks = []
    for c in range(2):
        for x in range(NPE - 1):
            block = field[last, c, x * 64 : x * 64 + 56, :]
            blocks.append(jnp.where(owned_z, block, 0.0))
    columns = jnp.concatenate(blocks, axis=0)
    high, low = split(columns)
    both = lax.dot_general(
        high,
        jnp.concatenate([high, low], axis=1),
        (((0,), (0,)), ((), ())),
        preferred_element_type=F32,
    )
    cross = both[:, STATES:]
    gram[...] = both[:, :STATES] + (cross + cross.T)

    piece = STATES // ring
    mine = pl.ds(pl.multiple_of(ring_place * piece, piece), piece)

    def scatter(j):
        rows = pl.ds(pl.multiple_of(lax.rem(ring_place + j, ring) * piece, piece), piece)
        return pltpu.make_async_remote_copy(
            src_ref=gram.at[rows],
            dst_ref=r_scatter.at[j - 1],
            send_sem=sum_send.at[0],
            recv_sem=sum_recv.at[0],
            device_id=in_ring(j),
            device_id_type=MESH,
        )

    def reduce(j):
        return pltpu.make_async_remote_copy(
            src_ref=r_reduce.at[other_place],
            dst_ref=r_reduce.at[other_place],
            send_sem=sum_send.at[1],
            recv_sem=sum_recv.at[1],
            device_id=across(j),
            device_id_type=MESH,
        )

    def gather(j):
        return pltpu.make_async_remote_copy(
            src_ref=r_gather.at[mine],
            dst_ref=r_gather.at[mine],
            send_sem=sum_send.at[2],
            recv_sem=sum_recv.at[2],
            device_id=in_ring(j),
            device_id_type=MESH,
        )

    def waiter(ref, k):
        return pltpu.make_async_remote_copy(
            src_ref=ref,
            dst_ref=ref,
            send_sem=sum_send.at[k],
            recv_sem=sum_recv.at[k],
            device_id=in_ring(1),
            device_id_type=MESH,
        )

    for j in range(1, ring):
        scatter(j).start()
    waiter(r_scatter, 0).wait_recv()
    r_reduce[other_place] = gram[mine, :] + jnp.sum(r_scatter[...], axis=0)
    for j in range(1, others):
        reduce(j).start()
    waiter(r_scatter, 0).wait_send()
    waiter(r_reduce.at[pl.ds(0, others - 1)], 1).wait_recv()
    nodes = 686 * nx * ny * nz
    r_gather[mine, :] = jnp.sum(r_reduce[...], axis=0) * (1.0 / nodes)
    for j in range(1, ring):
        gather(j).start()
    waiter(r_reduce.at[pl.ds(0, others - 1)], 1).wait_send()
    rest = r_gather.at[pl.ds(0, piece * (ring - 1))]
    waiter(rest, 2).wait_recv()

    total = r_gather[...]
    diagonal = lax.broadcasted_iota(jnp.int32, (STATES, STATES), 0) == (
        lax.broadcasted_iota(jnp.int32, (STATES, STATES), 1)
    )
    trace = jnp.sum(jnp.where(diagonal, total, 0.0), keepdims=True)
    three = jnp.where(diagonal, 3.0, 0.0)

    def newton(k, pair):
        root, inverse = pair
        middle = three - product(inverse, root)
        return 0.5 * product(root, middle), 0.5 * product(middle, inverse)

    scaled = total / trace
    middle = three - scaled
    root, inverse = lax.fori_loop(
        0, NS_STEPS - 2, newton, (0.5 * product(scaled, middle), 0.5 * middle)
    )
    inverse = 0.5 * product(three - product(inverse, root), inverse)
    rotation = inverse / jnp.sqrt(trace)
    for c in range(2):
        for x in range(NPE - 1):
            turned = product(field[last, c, x * 64 : x * 64 + 56, :], rotation)
            for y in range(NPE - 1):
                out_ref[x, y, c * 7 : c * 7 + 7, :] = turned[y * 8 : y * 8 + 7, :]
    waiter(rest, 2).wait_send()


def shards(wavefunctions, hamiltonians, cell_order):
    sizes = tuple(lax.axis_size(a) for a in AXES)
    ring, others = sizes[0] * 2, sizes[1] // 2 * sizes[2]
    piece = STATES // ring
    matrices = hamiltonians.reshape((2, CDOF, CDOF))
    orders = cell_order.reshape((2, CDOF))
    kinds = len(KINDS)
    return pl.pallas_call(
        functools.partial(kernel, sizes),
        out_shape=pltpu.VMEM(wavefunctions.shape, F32),
        in_specs=[pl.BlockSpec(memory_space=pltpu.HBM)] * 3,
        out_specs=pl.BlockSpec(memory_space=pltpu.VMEM),
        scratch_shapes=[
            pltpu.VMEM(wavefunctions.shape, F32),
            pltpu.VMEM((2, CDOF, CDOF), F32),
            pltpu.VMEM((2, ROWS, CDOF), BF16),
            pltpu.VMEM((2, EARLY, CDOF), BF16),
            pltpu.VMEM((2, LATE, CDOF), BF16),
            pltpu.VMEM((2, CDOF), jnp.int32),
            pltpu.VMEM((2, 2 * ROWS, EARLY), BF16),
            pltpu.VMEM((2, 2 * SENT, LATE), BF16),
            pltpu.VMEM((2, 2 * INNER, LATE), BF16),
            pltpu.VMEM((2, ROWS, STATES), F32),
            pltpu.VMEM((2, 2, CDOF, STATES), F32),
            pltpu.VMEM((2, 64, STATES), F32),
            pltpu.VMEM((2, 256, STATES), F32),
            pltpu.VMEM((2, INNER + 32, STATES), F32),
            pltpu.VMEM((2, 2, 8, STATES), F32),
            pltpu.VMEM((2, 2, 2, 64, STATES), F32),
            pltpu.VMEM((2, 2, 2, 64, STATES), F32),
            pltpu.VMEM((2, 2, 64, STATES), F32),
            pltpu.VMEM((2, 4, 2, 8, STATES), F32),
            pltpu.VMEM((2, 4, 8, STATES), F32),
            pltpu.VMEM((2, 4, 8, STATES), F32),
            pltpu.VMEM((2, 8, STATES), F32),
            pltpu.VMEM((STATES, STATES), F32),
            pltpu.VMEM((ring - 1, piece, STATES), F32),
            pltpu.VMEM((others, piece, STATES), F32),
            pltpu.VMEM((STATES, STATES), F32),
            pltpu.SemaphoreType.DMA((4,)),
            pltpu.SemaphoreType.DMA((kinds,)),
            pltpu.SemaphoreType.DMA((2, 2 + kinds)),
            pltpu.SemaphoreType.DMA((3,)),
            pltpu.SemaphoreType.DMA((3,)),
        ],
        compiler_params=pltpu.CompilerParams(
            collective_id=0, has_side_effects=True, vmem_limit_bytes=56 << 20
        ),
    )(wavefunctions, matrices, orders)


def solution(mesh):
    in_specs = (
        P("gx", "gy", "gz", None),
        P("gx", "gy", "gz", None, None),
        P("gx", "gy", "gz", None),
    )
    out_specs = P("gx", "gy", "gz", None)
    return jax.shard_map(
        shards, mesh=mesh, in_specs=in_specs, out_specs=out_specs, check_vma=False
    )
```

profile of v0, /device:TPU:1, one launch (start us, length us, event | category | flops | bytes accessed | tf_op | source)
XLA Modules:
  0.0 64.9 jit_solution(9656650284118980266)
XLA Ops:
  0.0 64.2 %shard_map.37 = f32[7,7,14,128]{3,2,1,0:T(8,128)S(1)} custom-call(f32[7,7,14,128]{3,2,1,0:T(8,128)} %wave_hbm.1, f32[2,512,512]{2,1,0:T(8,128)} %bitcast.2, s32[2,512]{1,0:T(2,128)} %bitcast.3), custom_call_target="tpu_custom_call" | custom-call | tf_op jit(solution)/shard_map/pallas_call | solution.py:531
  64.2 0.8 %copy.5 = f32[7,7,14,128]{3,2,1,0:T(8,128)} copy(f32[7,7,14,128]{3,2,1,0:T(8,128)S(1)} %shard_map.37) | data formatting | bytes 702464
where the time goes:
time: 65 us; the launch traced here: 64.9 us
  Pallas kernels  64.2 us (99%)
  local copies, waits for them, and re-layouts  0.75 us (1%)
    pallas_call x1, Pallas kernels, shards(): pl.pallas_call(functools.partial(kernel, sizes), out_shape=pltpu.VMEM(wav...  64.2 us

commit v1 on v0

--- a/solution.py
+++ b/solution.py
@@ -24,8 +24,8 @@
     (d for d in itertools.product((-1, 0, 1), repeat=3) if any(d)),
     key=lambda d: -sum(map(abs, d)),
 )
-DOWN = [d for d in itertools.product((-1, 0), repeat=3) if any(d)]
-UP = [d for d in itertools.product((1, 0), repeat=3) if any(d)]
+DOWN = [d for d in ALL if max(d) <= 0]
+UP = [d for d in ALL if min(d) >= 0]
 
 KINDS = ("x", "z", "xz", "y", "xy", "yz", "xyz")
 Y_ROWS, X_ROWS = 0, 128
@@ -118,13 +118,19 @@
     other_place = (me[1] // 2) * nz + me[2]
     ring, others = nx * 2, (ny // 2) * nz
 
+    def turns(*lengths):
+        shifts = [j for j in itertools.product(*map(range, lengths)) if any(j)]
+        return sorted(shifts, key=lambda j: -sum(min(i, n - i) for i, n in zip(j, lengths)))
+
     def in_ring(j):
-        place = lax.rem(ring_place + j, ring)
-        return (place // 2, (me[1] // 2) * 2 + lax.rem(place, 2), me[2])
+        x = lax.rem(me[0] + j[0], nx)
+        core = lax.rem(me[1] + j[1], 2)
+        return (x, (me[1] // 2) * 2 + core, me[2]), x * 2 + core
 
     def across(j):
-        place = lax.rem(other_place + j, others)
-        return (me[0], (place // nz) * 2 + lax.rem(me[1], 2), lax.rem(place, nz))
+        y = lax.rem((me[1] // 2) * 2 + me[2] // 4 + j[0], 4)
+        z = lax.rem(y, 2) * 4 + lax.rem(me[2] + j[1], 4)
+        return (me[0], (y // 2) * 2 + lax.rem(me[1], 2), z)
 
     barrier = pltpu.get_barrier_semaphore()
     for d in UP + DOWN:
@@ -349,19 +355,23 @@
         later = slot = 1 - now
         gain, shift = factor / HALF_WIDTH, -factor * CENTER / HALF_WIDTH
         values = [late_values(now, c) for c in range(2)]
+        products = []
         for c in range(2):
-            products = early[c, :SENT, :] + four(ham_sent[c], values[c])
-            rims[c] = products[:64]
-            faces[c, Y_ROWS : Y_ROWS + 128, :] = products[64:192]
+            products.append(early[c, :SENT, :] + four(ham_sent[c], values[c]))
+            rims[c] = products[c][:64]
+        pack_yz()
+        first = [d for d in directions if kind_of(d) in ("xz", "yz", "xyz")]
+        send(first, slot)
+        for c in range(2):
+            faces[c, Y_ROWS : Y_ROWS + 128, :] = products[c][64:192]
             for t in range(2):
                 row = X_ROWS + t * 64
-                faces[c, row + 8 : row + 56, :] = products[192 + t * 48 : 240 + t * 48]
+                faces[c, row + 8 : row + 56, :] = products[c][192 + t * 48 : 240 + t * 48]
                 for u in range(2):
-                    edge = products[64 + u * 64 + t * 56 : 72 + u * 64 + t * 56]
+                    edge = products[c][64 + u * 64 + t * 56 : 72 + u * 64 + t * 56]
                     faces[c, row + u * 56 : row + u * 56 + 8, :] = edge
-        pack_yz()
         join(faces, 0, 32)
-        send(directions, slot)
+        send([d for d in directions if d not in first], slot)
         for c in range(2):
             inner[c, :INNER, :] = early[c, SENT:, :] + four(ham_inner[c], values[c])
         join(inner, 0, 36)
@@ -388,24 +398,25 @@
         if directions is ALL:
             collect_y(total, slot, near_place, gain)
             multiply_early(later)
+            wait_sent(directions, slot)
             collect(total, [d for d in ALL if kind_of(d) != "y"], slot, gain)
             collect_y(total, slot, 1 - near_place, gain)
         else:
+            wait_sent(directions, slot)
             collect(total, directions, slot, gain)
-        wait_sent(directions, slot)
 
     @pl.when(near_place == 0)
     def _():
         collect_y(field.at[0], 0, 0, 1.0)
 
     multiply_early(0)
+    wait_sent(DOWN, 0)
     collect(field.at[0], [d for d in DOWN if kind_of(d) != "y"], 0, 1.0)
 
     @pl.when(near_place == 1)
     def _():
         collect_y(field.at[0], 0, 0, 1.0)
 
-    wait_sent(DOWN, 0)
     apply(0, ALL, 1.0, False)
 
     def two_steps(k, carry):
@@ -437,14 +448,15 @@
     piece = STATES // ring
     mine = pl.ds(pl.multiple_of(ring_place * piece, piece), piece)
 
-    def scatter(j):
-        rows = pl.ds(pl.multiple_of(lax.rem(ring_place + j, ring) * piece, piece), piece)
+    def scatter(k, j):
+        device, place = in_ring(j)
+        rows = pl.ds(pl.multiple_of(place * piece, piece), piece)
         return pltpu.make_async_remote_copy(
             src_ref=gram.at[rows],
-            dst_ref=r_scatter.at[j - 1],
+            dst_ref=r_scatter.at[k],
             send_sem=sum_send.at[0],
             recv_sem=sum_recv.at[0],
-            device_id=in_ring(j),
+            device_id=device,
             device_id_type=MESH,
         )
 
@@ -464,7 +476,7 @@
             dst_ref=r_gather.at[mine],
             send_sem=sum_send.at[2],
             recv_sem=sum_recv.at[2],
-            device_id=in_ring(j),
+            device_id=in_ring(j)[0],
             device_id_type=MESH,
         )
 
@@ -474,21 +486,21 @@
             dst_ref=ref,
             send_sem=sum_send.at[k],
             recv_sem=sum_recv.at[k],
-            device_id=in_ring(1),
-            device_id_type=MESH,
-        )
-
-    for j in range(1, ring):
-        scatter(j).start()
+            device_id=neighbour((1, 0, 0)),
+            device_id_type=MESH,
+        )
+
+    for k, j in enumerate(turns(nx, 2)):
+        scatter(k, j).start()
     waiter(r_scatter, 0).wait_recv()
     r_reduce[other_place] = gram[mine, :] + jnp.sum(r_scatter[...], axis=0)
-    for j in range(1, others):
+    for j in turns(4, 4):
         reduce(j).start()
     waiter(r_scatter, 0).wait_send()
     waiter(r_reduce.at[pl.ds(0, others - 1)], 1).wait_recv()
     nodes = 686 * nx * ny * nz
     r_gather[mine, :] = jnp.sum(r_reduce[...], axis=0) * (1.0 / nodes)
-    for j in range(1, ring):
+    for j in turns(nx, 2):
         gather(j).start()
     waiter(r_reduce.at[pl.ds(0, others - 1)], 1).wait_send()
     rest = r_gather.at[pl.ds(0, piece * (ring - 1))]

time: 65 us -> 64.3 us (0.989)
  Pallas kernels: 64.2 us -> 63.5 us
    pallas_call x1, Pallas kernels: 64.2 us -> 63.5 us  [shards(): pl.pallas_call(functools.partial(kernel, sizes), out_shape=pltpu.VMEM(wav...]
where the time goes in v1:
time: 64.3 us; the launch traced here: 64.2 us
  Pallas kernels  63.5 us (99%)
  local copies, waits for them, and re-layouts  0.75 us (1%)
    pallas_call x1, Pallas kernels, shards(): pl.pallas_call(functools.partial(kernel, sizes), out_shape=pltpu.VMEM(wav...  63.5 us

profile of v1, /device:TPU:1, one launch (start us, length us, event | category | flops | bytes accessed | tf_op | source)
XLA Modules:
  0.0 64.2 jit_solution(18354281923253528668)
XLA Ops:
  0.0 63.5 %shard_map.37 = f32[7,7,14,128]{3,2,1,0:T(8,128)S(1)} custom-call(f32[7,7,14,128]{3,2,1,0:T(8,128)} %wave_hbm.1, f32[2,512,512]{2,1,0:T(8,128)} %bitcast.2, s32[2,512]{1,0:T(2,128)} %bitcast.3), custom_call_target="tpu_custom_call" | custom-call | tf_op jit(solution)/shard_map/pallas_call | solution.py:543
  63.5 0.8 %copy.5 = f32[7,7,14,128]{3,2,1,0:T(8,128)} copy(f32[7,7,14,128]{3,2,1,0:T(8,128)S(1)} %shard_map.37) | data formatting | bytes 702464

commit v2 on v1

--- a/solution.py
+++ b/solution.py
@@ -23,6 +23,11 @@
 ALL = sorted(
     (d for d in itertools.product((-1, 0, 1), repeat=3) if any(d)),
     key=lambda d: -sum(map(abs, d)),
+)
+NEAR, FAR = 1, 2
+CODED = sorted(
+    (d for d in itertools.product((-1, 0, 1), (0, NEAR, FAR), (-1, 0, 1)) if any(d)),
+    key=lambda d: (-sum(map(bool, d)), (1, 2, 0)[d[1]]),
 )
 DOWN = [d for d in ALL if max(d) <= 0]
 UP = [d for d in ALL if min(d) >= 0]
@@ -90,6 +95,7 @@
     r_xz,
     r_yz,
     r_xyz,
+    parts,
     gram,
     r_scatter,
     r_reduce,
@@ -111,6 +117,9 @@
         d: tuple(table[s] for table, s in zip(shifted, d)) for d in ALL
     }
 
+    core = lax.rem(me[1], 2)
+    coded_y = {0: me[1], NEAR: me[1] + 1 - 2 * core, FAR: lax.rem(me[1] + 2 * core + 3, 4)}
+
     def neighbour(d):
         return neighbours[d]
 
@@ -145,10 +154,13 @@
     for load in loads:
         load.start()
 
-    def message(d, slot):
+    def message(d, slot, coded):
         dx, dy, dz = d
         kind = kind_of(d)
         sx, sy, sz = side(dx), side(dy), side(dz)
+        device = neighbours[d] if not coded else (shifted[0][dx], coded_y[dy], shifted[2][dz])
+        if coded and dy:
+            sy = core if dy == FAR else 1 - core
         if kind == "x":
             source, place = faces.at[:, pl.ds(X_ROWS + sx * 64, 64)], sx
         elif kind == "y":
@@ -176,13 +188,13 @@
             dst_ref=target,
             send_sem=send_sem.at[k],
             recv_sem=recv_sem.at[slot, place if kind == "y" else 2 + k],
-            device_id=neighbour(d),
+            device_id=device,
             device_id_type=MESH,
         )
 
-    def send(directions, slot):
+    def send(directions, slot, coded=False):
         for d in directions:
-            message(d, slot).start()
+            message(d, slot, coded).start()
 
     def every(kind, directions, slot):
         count = sum(kind_of(d) == kind for d in directions)
@@ -267,31 +279,37 @@
     loads[1].wait()
     near_place = lax.rem(me[1], 2)
     near_y = 7 * (1 - near_place)
-    row_of = lax.broadcasted_iota(jnp.int32, (CDOF, CDOF), 0)
-    n = lax.broadcasted_iota(jnp.int32, (64, CDOF), 0)
+    lanes = 128
+    row_of = lax.broadcasted_iota(jnp.int32, (CDOF, lanes), 0)
+    n, k = row_of[:64], row_of[:48]
+    none = jnp.full((48, lanes), -1, jnp.int32)
     for c in range(2):
         order = order_ref[c : c + 1, :]
 
         def chosen(rows):
-            return (rows == order).astype(F32).astype(BF16)
-
-        block = (n // 8) * 64 + lax.rem(n, 8)
+            return jnp.concatenate(
+                [
+                    (rows == order[:, first : first + lanes]).astype(F32).astype(BF16)
+                    for first in range(0, CDOF, lanes)
+                ],
+                axis=1,
+            )
+
+        block = (n >> 3) * 64 + (n & 7)
         rows = [n * 8 + 7 * c, block, block + 56, n[8:56], n[8:56] + 448]
         rows += [row_of[x * 64 + 8 : x * 64 + 56] for x in range(1, NPE - 1)]
         pick[c] = chosen(jnp.concatenate(rows, axis=0))
-        k = lax.broadcasted_iota(jnp.int32, (48, CDOF), 0)
-        none = jnp.full((48, CDOF), -1, jnp.int32)
-        near_rows = (k // 8 + 1) * 64 + near_y * 8 + lax.rem(k, 8)
+        near_rows = ((k >> 3) + 1) * 64 + near_y * 8 + (k & 7)
         early_rows = [row_of[x * 64 + 8 : x * 64 + 56] for x in range(1, NPE - 1)]
         early_rows = [
-            jnp.where(lax.rem(k, 8) == 7 * c, -1, rows) for rows in early_rows + [near_rows]
+            jnp.where((k & 7) == 7 * c, -1, rows) for rows in early_rows + [near_rows]
         ] + [none]
-        rim_rows = (k // 8 + 1) * 64 + lax.rem(k, 8) * 8 + 7 * c
+        rim_rows = ((k >> 3) + 1) * 64 + (k & 7) * 8 + 7 * c
         late_rows = [
             n,
             n + 448,
-            (k // 8 + 1) * 64 + (7 - near_y) * 8 + lax.rem(k, 8),
-            jnp.where(lax.rem(k, 8) == 7 - near_y, -1, rim_rows),
+            ((k >> 3) + 1) * 64 + (7 - near_y) * 8 + (k & 7),
+            jnp.where((k & 7) == 7 - near_y, -1, rim_rows),
             none[:32],
         ]
         early_columns[c] = chosen(jnp.concatenate(early_rows, axis=0))
@@ -360,8 +378,10 @@
             products.append(early[c, :SENT, :] + four(ham_sent[c], values[c]))
             rims[c] = products[c][:64]
         pack_yz()
-        first = [d for d in directions if kind_of(d) in ("xz", "yz", "xyz")]
-        send(first, slot)
+        coded = directions is ALL
+        order = CODED if coded else directions
+        first = [d for d in order if kind_of(d) in ("xz", "yz", "xyz")]
+        send(first, slot, coded)
         for c in range(2):
             faces[c, Y_ROWS : Y_ROWS + 128, :] = products[c][64:192]
             for t in range(2):
@@ -371,7 +391,7 @@
                     edge = products[c][64 + u * 64 + t * 56 : 72 + u * 64 + t * 56]
                     faces[c, row + u * 56 : row + u * 56 + 8, :] = edge
         join(faces, 0, 32)
-        send([d for d in directions if d not in first], slot)
+        send([d for d in order if d not in first], slot, coded)
         for c in range(2):
             inner[c, :INNER, :] = early[c, SENT:, :] + four(ham_inner[c], values[c])
         join(inner, 0, 36)
@@ -436,9 +456,10 @@
             blocks.append(jnp.where(owned_z, block, 0.0))
     columns = jnp.concatenate(blocks, axis=0)
     high, low = split(columns)
+    parts[...] = jnp.concatenate([high, low], axis=1)
     both = lax.dot_general(
         high,
-        jnp.concatenate([high, low], axis=1),
+        parts[...],
         (((0,), (0,)), ((), ())),
         preferred_element_type=F32,
     )
@@ -524,12 +545,18 @@
         0, NS_STEPS - 2, newton, (0.5 * product(scaled, middle), 0.5 * middle)
     )
     inverse = 0.5 * product(three - product(inverse, root), inverse)
-    rotation = inverse / jnp.sqrt(trace)
+    high, low = split(inverse / jnp.sqrt(trace))
+    upper = jnp.concatenate([high, low], axis=1)
+    lower = jnp.concatenate([high, jnp.zeros_like(low)], axis=1)
+    both = jnp.dot(
+        parts[...], jnp.concatenate([upper, lower], axis=0), preferred_element_type=F32
+    )
+    turned = both[:, :STATES] + both[:, STATES:]
     for c in range(2):
         for x in range(NPE - 1):
-            turned = product(field[last, c, x * 64 : x * 64 + 56, :], rotation)
             for y in range(NPE - 1):
-                out_ref[x, y, c * 7 : c * 7 + 7, :] = turned[y * 8 : y * 8 + 7, :]
+                row = ((c * 7 + x) * 7 + y) * 8
+                out_ref[x, y, c * 7 : c * 7 + 7, :] = turned[row : row + 7]
     waiter(rest, 2).wait_send()
 
 
@@ -568,6 +595,7 @@
             pltpu.VMEM((2, 4, 8, STATES), F32),
             pltpu.VMEM((2, 4, 8, STATES), F32),
             pltpu.VMEM((2, 8, STATES), F32),
+            pltpu.VMEM((2 * 7 * 7 * 8, 2 * STATES), BF16),
             pltpu.VMEM((STATES, STATES), F32),
             pltpu.VMEM((ring - 1, piece, STATES), F32),
             pltpu.VMEM((others, piece, STATES), F32),

time: 64.3 us -> 64.2 us (level)
  no operation moved by 1% of the time
where the time goes in v2:
time: 64.2 us; the launch traced here: 64 us
  Pallas kernels  63.3 us (99%)
  local copies, waits for them, and re-layouts  0.75 us (1%)
    pallas_call x1, Pallas kernels, shards(): pl.pallas_call(functools.partial(kernel, sizes), out_shape=pltpu.VMEM(wav...  63.3 us

profile of v2, /device:TPU:1, one launch (start us, length us, event | category | flops | bytes accessed | tf_op | source)
XLA Modules:
  0.0 64.0 jit_solution(6774990515288067337)
XLA Ops:
  0.0 63.3 %shard_map.37 = f32[7,7,14,128]{3,2,1,0:T(8,128)S(1)} custom-call(f32[7,7,14,128]{3,2,1,0:T(8,128)} %wave_hbm.1, f32[2,512,512]{2,1,0:T(8,128)} %bitcast.2, s32[2,512]{1,0:T(2,128)} %bitcast.3), custom_call_target="tpu_custom_call" | custom-call | tf_op jit(solution)/shard_map/pallas_call | solution.py:570
  63.3 0.8 %copy.5 = f32[7,7,14,128]{3,2,1,0:T(8,128)} copy(f32[7,7,14,128]{3,2,1,0:T(8,128)S(1)} %shard_map.37) | data formatting | bytes 702464

commit v3 on v2

--- a/solution.py
+++ b/solution.py
@@ -369,6 +369,38 @@
         parts += [field[now, c, pl.ds(64 + 7 * c, 48, stride=8), :]]
         return pair(parts + [jnp.zeros((32, STATES), F32)])
 
+    def gram_of(columns):
+        high, low = split(columns)
+        both = lax.dot_general(
+            high,
+            jnp.concatenate([high, low], axis=1),
+            (((0,), (0,)), ((), ())),
+            preferred_element_type=F32,
+        )
+        cross = both[:, STATES:]
+        return both[:, :STATES] + (cross + cross.T)
+
+    sublane = lax.broadcasted_iota(jnp.int32, (56, STATES), 0) & 7
+
+    def inner_rows(now):
+        rows = []
+        for c in range(2):
+            kept = sublane[:48] < 7 if c else (sublane[:48] > 0) & (sublane[:48] < 7)
+            for x in range(1, NPE - 1):
+                rows.append(jnp.where(kept, field[now, c, x * 64 + 8 : x * 64 + 56, :], 0.0))
+        return jnp.concatenate(rows, axis=0)
+
+    def rim_rows_of(now):
+        rows = []
+        for c in range(2):
+            rows.append(jnp.where(sublane < 7, field[now, c, 0:56, :], 0.0))
+            for x in range(1, NPE - 1):
+                block = field[now, c, x * 64 : x * 64 + 8, :]
+                rows.append(jnp.where(sublane[:8] < 7, block, 0.0))
+        kept = (sublane[:48] > 0) & (sublane[:48] < 7)
+        rows.append(jnp.where(kept, field[now, 0, pl.ds(64, 48, stride=8), :], 0.0))
+        return jnp.concatenate(rows, axis=0)
+
     def apply(now, directions, factor, keep):
         later = slot = 1 - now
         gain, shift = factor / HALF_WIDTH, -factor * CENTER / HALF_WIDTH
@@ -422,6 +454,7 @@
             collect(total, [d for d in ALL if kind_of(d) != "y"], slot, gain)
             collect_y(total, slot, 1 - near_place, gain)
         else:
+            gram[...] = gram_of(inner_rows(later))
             wait_sent(directions, slot)
             collect(total, directions, slot, gain)
 
@@ -448,23 +481,7 @@
     apply(1, UP, 2.0, True)
     last = 0
 
-    owned_z = lax.broadcasted_iota(jnp.int32, (7 * 8, STATES), 0) % 8 < 7
-    blocks = []
-    for c in range(2):
-        for x in range(NPE - 1):
-            block = field[last, c, x * 64 : x * 64 + 56, :]
-            blocks.append(jnp.where(owned_z, block, 0.0))
-    columns = jnp.concatenate(blocks, axis=0)
-    high, low = split(columns)
-    parts[...] = jnp.concatenate([high, low], axis=1)
-    both = lax.dot_general(
-        high,
-        parts[...],
-        (((0,), (0,)), ((), ())),
-        preferred_element_type=F32,
-    )
-    cross = both[:, STATES:]
-    gram[...] = both[:, :STATES] + (cross + cross.T)
+    gram[...] += gram_of(rim_rows_of(last))
 
     piece = STATES // ring
     mine = pl.ds(pl.multiple_of(ring_place * piece, piece), piece)
@@ -513,6 +530,8 @@
 
     for k, j in enumerate(turns(nx, 2)):
         scatter(k, j).start()
+    blocks = [field[last, c, x * 64 : x * 64 + 56, :] for c in range(2) for x in range(NPE - 1)]
+    parts[...] = jnp.concatenate(split(jnp.concatenate(blocks, axis=0)), axis=1)
     waiter(r_scatter, 0).wait_recv()
     r_reduce[other_place] = gram[mine, :] + jnp.sum(r_scatter[...], axis=0)
     for j in turns(4, 4):

time: 64.2 us -> 64 us (level)
  no operation moved by 1% of the time
where the time goes in v3:
time: 64 us; the launch traced here: 63.9 us
  Pallas kernels  63.1 us (99%)
  local copies, waits for them, and re-layouts  0.75 us (1%)
    pallas_call x1, Pallas kernels, shards(): pl.pallas_call(functools.partial(kernel, sizes), out_shape=pltpu.VMEM(wav...  63.1 us

profile of v3, /device:TPU:1, one launch (start us, length us, event | category | flops | bytes accessed | tf_op | source)
XLA Modules:
  0.0 63.9 jit_solution(368866797096303568)
XLA Ops:
  0.0 63.1 %shard_map.37 = f32[7,7,14,128]{3,2,1,0:T(8,128)S(1)} custom-call(f32[7,7,14,128]{3,2,1,0:T(8,128)} %wave_hbm.1, f32[2,512,512]{2,1,0:T(8,128)} %bitcast.2, s32[2,512]{1,0:T(2,128)} %bitcast.3), custom_call_target="tpu_custom_call" | custom-call | tf_op jit(solution)/shard_map/pallas_call | solution.py:589
  63.1 0.8 %copy.5 = f32[7,7,14,128]{3,2,1,0:T(8,128)} copy(f32[7,7,14,128]{3,2,1,0:T(8,128)S(1)} %shard_map.37) | data formatting | bytes 702464
